TPU v7x, 32 devices: a whole 2x2x4 slice. The times are simulated.
32 devices in a mesh: seq: 8 (over z, y), head: 4 (over x, core).
Axes of the slice: x: 2, y: 2, z: 4, core: 2. Of those that a mesh axis runs over, the one named last changes fastest.
Arguments:
- hidden: bfloat16 [1024, 1024], P('seq', 'head'), may hold values from -6 to 6
- queries: bfloat16 [1024, 1024], P('seq', 'head'), may hold values from -40 to 40
- suffix_keys: bfloat16 [1024, 1024], P('seq', 'head'), may hold values from -4 to 4
- suffix_values: bfloat16 [1024, 1024], P('seq', 'head'), may hold values from -6 to 6
- lengths: int32 [8], P('seq'), may hold values from 1 to 128, 640 in all
- key_cache: bfloat16 [8, 32, 1024], P('seq', None, 'head'), may hold values from -6 to 6
- value_cache: bfloat16 [8, 32, 1024], P('seq', None, 'head'), may hold values from -6 to 6
- page_group: int32 [8], replicated, may hold values from 0 to 3, as said below
- out_weight: bfloat16 [1024, 1024], P('head'), may hold values from -0.1875 to 0.1875
- norm_gain: float32 [1024], replicated, may hold values from 0.1 to 1.9
- router_weight: bfloat16 [1024, 16], P('head'), may hold values from -0.1875 to 0.1875
- routes: int32 [1024, 2], P('seq'), may hold values from 0 to 15, all different within a row; in each aligned block of 128 rows (0 to 127, 128 to 255, ...) at most 20 rows name the same one
- gate_weight: bfloat16 [16, 1024, 2816], P('seq', None, 'head'), as said below
- up_weight: bfloat16 [16, 1024, 2816], P('seq', None, 'head'), as said below
- down_weight: bfloat16 [16, 1024, 2816], P('seq', None, 'head'), as said below
- destinations: int32 [8], replicated, may hold values from 0 to 7, as said below
Outputs:
- layer_output: bfloat16 [1024, 1024], P('seq', 'head')
Inputs may be any that keep to these rules, and one draw needn't show every extreme that they name: `lengths`: the largest length is 128. `page_group`: each of the 4 groups is named by exactly 2 entries. `routes`: each row names 2 different experts; in each aligned block of 128 rows no expert is named by more than 20 rows. `gate_weight`: copies h and h2 with h == h2 // 1 are equal. `up_weight`: copies h and h2 with h == h2 // 1 are equal. `down_weight`: copies h and h2 with h == h2 // 1 are equal. `destinations`: A permutation of the requests in which exactly 2 requests change place.
All inputs are finite; a program needn't handle non-finite values. No bound on the sum of `lengths` on one device may be relied on, other than what follows from the above.
Results may differ from a plain program's by a relative error of at most 0.0065.
Values may be sent and summed in bfloat16 or wider, within the bound.
A program may use at most 64 MiB of HBM per device.

v0:
```python
import jax
import jax.numpy as jnp
from jax import lax
from jax.sharding import PartitionSpec as P

DH = 64
EXPERTS = 16
TOPK = 2
GROUPS = 4


norm_eps = 1e-06


def page_inverse(page_group, group_pages, groups):
    page_total = page_group.shape[0]
    onehot = (page_group[:, None] == jnp.arange(groups, dtype=jnp.int32)[None, :]).astype(jnp.int32)
    page_rank = jnp.sum((jnp.cumsum(onehot, axis=0) - 1) * onehot, axis=1)
    target = page_group * group_pages + page_rank
    return (
        jnp.zeros((page_total,), jnp.int32).at[target].set(jnp.arange(page_total, dtype=jnp.int32))
    )


def attend_rows(query_rows, key_rows, value_rows, prefix_keys, prefix_values, length, head_total):
    row_count = query_rows.shape[0]
    head_size = query_rows.shape[1] // head_total
    scale = head_size ** (-0.5)

    def heads_of(array):
        return array.reshape(array.shape[0], head_total, head_size)

    prefix_scores = (
        jnp.einsum(
            "qhd,khd->hqk",
            heads_of(query_rows),
            heads_of(prefix_keys),
            preferred_element_type=jnp.float32,
        )
        * scale
    )
    suffix_scores = (
        jnp.einsum(
            "qhd,khd->hqk",
            heads_of(query_rows),
            heads_of(key_rows),
            preferred_element_type=jnp.float32,
        )
        * scale
    )
    query_pos = jnp.arange(row_count, dtype=jnp.int32)[:, None]
    key_pos = jnp.arange(row_count, dtype=jnp.int32)[None, :]
    allowed = (key_pos <= query_pos) & (key_pos < length)
    suffix_scores = jnp.where(allowed[None], suffix_scores, -jnp.inf)
    row_max = jnp.maximum(jnp.max(prefix_scores, axis=2), jnp.max(suffix_scores, axis=2))[..., None]
    prefix_exp = jnp.exp(prefix_scores - row_max)
    suffix_exp = jnp.exp(suffix_scores - row_max)
    denominators = jnp.sum(prefix_exp, axis=2, keepdims=True) + jnp.sum(
        suffix_exp, axis=2, keepdims=True
    )
    prefix_probs = (prefix_exp / denominators).astype(jnp.bfloat16)
    suffix_probs = (suffix_exp / denominators).astype(jnp.bfloat16)
    mixed_heads = jnp.einsum(
        "hqk,khd->qhd", prefix_probs, heads_of(prefix_values), preferred_element_type=jnp.float32
    )
    mixed_heads = mixed_heads + jnp.einsum(
        "hqk,khd->qhd", suffix_probs, heads_of(value_rows), preferred_element_type=jnp.float32
    )
    return mixed_heads.reshape(row_count, head_total * head_size).astype(jnp.bfloat16)


def slot_table(route_rows, replicas, per_device, experts):
    row_count, topk_count = route_rows.shape
    sub_rows = row_count // replicas
    flat_routes = route_rows.reshape(replicas, sub_rows * topk_count)
    onehot = (flat_routes[..., None] == jnp.arange(experts, dtype=jnp.int32)).astype(jnp.int32)
    slot_rank = jnp.sum((jnp.cumsum(onehot, axis=1) - 1) * onehot, axis=2).reshape(-1)
    expert_flat = route_rows.reshape(-1)
    block_of = jnp.arange(row_count * topk_count, dtype=jnp.int32) // (sub_rows * topk_count)
    target_device = expert_flat // per_device * replicas + block_of
    local_slot = expert_flat % per_device
    return (target_device, local_slot, slot_rank)


def on_device(
    hidden,
    queries,
    suffix_keys,
    suffix_values,
    lengths,
    key_cache,
    value_cache,
    page_group,
    out_weight,
    norm_gain,
    router_weight,
    routes,
    gate_weight,
    up_weight,
    down_weight,
    destinations,
):
    seq_count = lax.axis_size("seq")
    head_count = lax.axis_size("head")
    seq_index = lax.axis_index("seq")
    head_index = lax.axis_index("head")
    row_count = hidden.shape[0]
    column_width = hidden.shape[1]
    features = queries.shape[1]
    local_heads = features // DH
    block_devices = seq_count // GROUPS
    page_local = key_cache.shape[0]
    page_rows = key_cache.shape[1]
    group_pages = page_local * block_devices
    replicas = max(1, seq_count // EXPERTS)
    per_device = max(1, EXPERTS // seq_count)
    capacity = 5 * row_count * TOPK // (4 * EXPERTS * replicas)
    inverse = page_inverse(page_group, group_pages, GROUPS)
    group_index = seq_index // block_devices
    half_width = page_rows * features
    local_pages = jnp.concatenate(
        [key_cache.reshape(page_local, half_width), value_cache.reshape(page_local, half_width)],
        axis=1,
    )
    all_pages = lax.all_gather(local_pages, "seq", axis=0, tiled=True)
    chosen = lax.dynamic_slice_in_dim(inverse, group_index * group_pages, group_pages, 0)
    held_pages = jnp.take(all_pages, chosen, axis=0)
    prefix_keys = held_pages[:, :half_width].reshape(group_pages * page_rows, features)
    prefix_values = held_pages[:, half_width:].reshape(group_pages * page_rows, features)
    length = lengths[0]
    attended = attend_rows(
        queries, suffix_keys, suffix_values, prefix_keys, prefix_values, length, local_heads
    )
    partial_proj = jnp.dot(attended, out_weight, preferred_element_type=jnp.float32)
    own_columns = lax.dynamic_slice_in_dim(
        partial_proj, head_index * column_width, column_width, 1
    ) + hidden.astype(jnp.float32)
    partial_proj = lax.dynamic_update_slice_in_dim(
        partial_proj, own_columns, head_index * column_width, 1
    )
    resid = lax.psum(partial_proj, "head")
    normed = (
        resid * lax.rsqrt(jnp.mean(resid * resid, axis=1, keepdims=True) + norm_eps) * norm_gain
    ).astype(jnp.bfloat16)
    normed_columns = lax.dynamic_slice_in_dim(normed, head_index * column_width, column_width, 1)
    logits = lax.psum(
        jnp.dot(normed_columns, router_weight, preferred_element_type=jnp.float32), "head"
    )
    chosen_logits = jnp.take_along_axis(logits, routes, axis=1)
    gate_first = jax.nn.sigmoid(chosen_logits[:, 0] - chosen_logits[:, 1])
    gate_second = jax.nn.sigmoid(chosen_logits[:, 1] - chosen_logits[:, 0])
    target_device, local_slot, slot_rank = slot_table(routes, replicas, per_device, EXPERTS)
    token_index = jnp.arange(row_count * TOPK, dtype=jnp.int32) // TOPK
    send_rows = jnp.zeros((seq_count, per_device, capacity, normed.shape[1]), jnp.bfloat16)
    send_rows = send_rows.at[target_device, local_slot, slot_rank].set(
        jnp.take(normed, token_index, axis=0)
    )
    slots = lax.all_to_all(send_rows, "seq", split_axis=0, concat_axis=0, tiled=True)
    gate_act = jnp.einsum("spnd,pdf->spnf", slots, gate_weight, preferred_element_type=jnp.float32)
    up_act = jnp.einsum("spnd,pdf->spnf", slots, up_weight, preferred_element_type=jnp.float32)
    expert_hidden = (jax.nn.gelu(gate_act, approximate=True) * up_act).astype(jnp.bfloat16)
    partial_out = jnp.einsum(
        "spnf,pdf->spnd", expert_hidden, down_weight, preferred_element_type=jnp.float32
    )
    part_dims = partial_out.shape
    split_part = partial_out.reshape(
        part_dims[0], part_dims[1], part_dims[2], head_count, part_dims[3] // head_count
    )
    arrived = lax.all_to_all(
        lax.all_to_all(
            split_part.astype(jnp.bfloat16), "seq", split_axis=0, concat_axis=0, tiled=True
        ),
        "head",
        split_axis=3,
        concat_axis=3,
        tiled=True,
    ).astype(split_part.dtype)
    returned = jnp.sum(arrived, axis=3).astype(jnp.bfloat16)
    picked = (
        returned[target_device, local_slot, slot_rank]
        .astype(jnp.float32)
        .reshape(row_count, TOPK, column_width)
    )
    resid_columns = lax.dynamic_slice_in_dim(resid, head_index * column_width, column_width, 1)
    layer = resid_columns + gate_first[:, None] * picked[:, 0] + gate_second[:, None] * picked[:, 1]
    layer = layer.astype(jnp.bfloat16)
    live_rows = jnp.arange(row_count, dtype=jnp.int32) < length
    layer = jnp.where(live_rows[:, None], layer, jnp.zeros_like(layer))
    out_pieces = layer.reshape(seq_count, row_count // seq_count, column_width)
    scattered = lax.all_to_all(out_pieces, "seq", split_axis=0, concat_axis=0, tiled=True)
    inverse_destination = (
        jnp.zeros((seq_count,), jnp.int32)
        .at[destinations]
        .set(jnp.arange(seq_count, dtype=jnp.int32))
    )
    reordered = jnp.take(scattered, inverse_destination, axis=0)
    settled = lax.all_to_all(reordered, "seq", split_axis=0, concat_axis=0, tiled=True)
    return settled.reshape(row_count, column_width)


def solution(mesh):
    return jax.shard_map(
        on_device,
        mesh=mesh,
        in_specs=(
            P("seq", "head"),
            P("seq", "head"),
            P("seq", "head"),
            P("seq", "head"),
            P("seq"),
            P("seq", None, "head"),
            P("seq", None, "head"),
            P(),
            P("head", None),
            P(),
            P("head", None),
            P("seq", None),
            P("seq", None, "head"),
            P("seq", None, "head"),
            P("seq", None, "head"),
            P(),
        ),
        out_specs=P("seq", "head"),
        check_vma=False,
    )
```

profile of v0, /device:TPU:0, one launch (start us, length us, event | category | flops | bytes accessed | tf_op | source)
XLA Modules:
  0.0 242.7 jit_solution(15931363385306843677)
XLA Ops:
  7.4 0.7 fusion.60
  8.1 0.2 reduce_window_sum.31
  8.3 0.7 select_reduce_fusion
  8.9 1.2 compare_select_fusion.8
  10.1 0.6 scatter_custom_fusion.1
  10.9 0.7 copy.170
  11.7 0.7 copy.171
  12.4 1.0 copy.138
  13.4 1.0 copy.140
  14.3 1.0 copy.142
  15.4 33.0 %all-gather = bf16[8,1,16384]{2,1,0:T(2,128)(2,1)S(1)} all-gather(bf16[1,1,16384]{2,1,0:T(2,128)(2,1)S(1)} %maximum_bitcast_fusion), channel_id=1, replica_groups=mesh['seq'=8,'head'=4] {'seq'}, dimensions={0}, use_global_device_ids=true | all-gather | bytes 294912 | tf_op jit(solution)/shard_map/all_gather | solution.py:125
  48.4 0.3 copy.202
  48.7 0.6 gather_fusion
  49.9 0.3 fusion.73
  50.3 0.2 convolution_bitcast_fusion.1
  50.7 0.6 copy-done.3
  51.3 0.2 fusion.74
  51.6 0.8 copy-done.2
  52.9 0.6 reduce-window.6
  54.0 32.9 %all-reduce.2.cloned.1.call-done = f32[128,1024]{1,0:T(8,128)} async-done(((f32[128,1024]{1,0:T(8,128)}), f32[128,1024]{1,0:T(8,128)}) %all-reduce.2.cloned.1.call-update) | async-done | bytes 524304 | tf_op jit(solution)/shard_map/psum | solution.py:141
  86.9 1.2 multiply_reduce_fusion
  88.1 1.2 multiply_convert_fusion
  89.3 2.0 gather_fusion.1
  91.2 1.9 broadcast_select_fusion
  93.2 1.2 broadcast_in_dim.100
  94.3 37.4 %scatter_fusion = bf16[8,2,20,1024]{3,1,2,0:T(2,128)(2,1)} fusion(bf16[8,2,20,1024]{3,1,2,0:T(2,128)(2,1)} %broadcast_in_dim.100, s32[256]{0:T(256)S(1)} %bitcast.128, bf16[256,1024]{1,0:T(8,128)(2,1)} %broadcast_select_fusion), kind=kCustom, calls=%fused_computation.7 | custom fusion | bytes 1575936 | tf_op jit(solution)/shard_map/scatter | solution.py:155
  131.7 22.2 %all_to_all.25 = bf16[8,2,20,1024]{3,1,2,0:T(2,128)(2,1)S(1)} all-to-all(bf16[8,2,20,1024]{3,1,2,0:T(2,128)(2,1)} %scatter_fusion), channel_id=1, replica_groups=mesh['seq'=8,'head'=4] {'seq'}, dimensions={0} | all-to-all | bytes 1310720 | tf_op jit(solution)/shard_map/all_to_all | solution.py:158
  154.0 0.8 copy-done.1
  154.8 4.0 %fusion.30 = f32[8,2,20,704]{3,2,0,1:T(8,128)} fusion(bf16[2,1024,704]{1,2,0:T(8,128)(2,1)} %param.28, bf16[8,2,20,1024]{3,1,2,0:T(2,128)(2,1)S(1)} %all_to_all.25), kind=kOutput, calls=%fused_computation.27 | convolution fusion | flops 463175680 | bytes 4440064 | tf_op jit(solution)/shard_map/spnd,pdf->spnf/dot_general | solution.py:159
  158.8 4.9 %fusion.21 = bf16[8,2,20,1024]{3,2,0,1:T(8,128)(2,1)} fusion(bf16[2,1024,704]{1,2,0:T(8,128)(2,1)S(1)} %copy-done, f32[8,2,20,704]{3,2,0,1:T(8,128)} %fusion.30, bf16[2,1024,704]{1,2,0:T(8,128)(2,1)} %param.29, bf16[8,2,20,1024]{3,1,2,0:T(2,128)(2,1)} %copy-done.1), kind=kOutput, calls=%fused_computation.20 | convolution fusion | flops 923525120 | bytes 7979008 | tf_op jit(solution)/shard_map/spnf,pdf->spnd/dot_general | solution.py:162
  163.8 2.5 %reshape.526 = bf16[8,2,20,4,256]{4,3,2,0,1:T(4,128)(2,1)} reshape(bf16[8,2,20,1024]{3,2,0,1:T(8,128)(2,1)} %fusion.21) | data formatting | bytes 1310720 | tf_op jit(solution)/shard_map/convert_element_type | solution.py:171
  166.3 2.2 copy.154
  168.4 4.2 %all-to-all-start.1 = ((bf16[8,2,20,4,256]{4,3,2,1,0:T(4,128)(2,1)}), bf16[8,2,20,4,256]{4,3,2,1,0:T(4,128)(2,1)}, u32[]{:S(2)}, u32[]{:S(2)}) async-start(bf16[8,2,20,4,256]{4,3,2,1,0:T(4,128)(2,1)} %copy.154), calls=%async_computation.1 | async-start | bytes 1310720 | tf_op jit(solution)/shard_map/all_to_all | solution.py:170
  172.9 0.7 scatter_custom_fusion
  173.7 14.9 %all-to-all-done.1 = bf16[8,2,20,4,256]{4,3,2,1,0:T(4,128)(2,1)} async-done(((bf16[8,2,20,4,256]{4,3,2,1,0:T(4,128)(2,1)}), bf16[8,2,20,4,256]{4,3,2,1,0:T(4,128)(2,1)}, u32[]{:S(2)}, u32[]{:S(2)}) %all-to-all-start.1) | async-done | bytes 655392 | tf_op jit(solution)/shard_map/all_to_all | solution.py:170
  188.6 2.3 copy.155
  190.9 4.2 %all-to-all-start.2 = ((bf16[8,2,20,4,256]{4,0,2,1,3:T(8,128)(2,1)}), bf16[8,2,20,4,256]{4,0,2,1,3:T(8,128)(2,1)}, u32[]{:S(2)}, u32[]{:S(2)}) async-start(bf16[8,2,20,4,256]{4,0,2,1,3:T(8,128)(2,1)} %copy.155), calls=%async_computation.2 | async-start | bytes 1310720 | tf_op jit(solution)/shard_map/all_to_all | solution.py:169
  195.2 11.9 %psum.15 = f32[128,16]{0,1:T(8,128)S(1)} all-reduce(f32[128,16]{0,1:T(8,128)S(1)} %fusion.54), channel_id=1, replica_groups=mesh['seq'=8,'head'=4] {'head'}, use_global_device_ids=true, to_apply=%region_10.11 | all-reduce | flops 2048 | bytes 16384 | tf_op jit(solution)/shard_map/psum | solution.py:146
  207.1 2.0 gather_fusion.4
  209.3 1.2 reduce_sum.65
  210.7 1.9 gather_fusion.2
  212.8 0.2 fusion.70
  213.0 1.7 fusion.51
  214.7 3.7 %all-to-all-start.3 = ((bf16[8,16,256]{2,1,0:T(8,128)(2,1)}), bf16[8,16,256]{2,1,0:T(8,128)(2,1)S(1)}, u32[]{:S(2)}, u32[]{:S(2)}) async-start(bf16[8,16,256]{2,1,0:T(8,128)(2,1)} %bitcast.33), calls=%async_computation.3 | async-start | bytes 131072 | tf_op jit(solution)/shard_map/all_to_all | solution.py:190
  218.4 6.9 %all-to-all-done.3 = bf16[8,16,256]{2,1,0:T(8,128)(2,1)S(1)} async-done(((bf16[8,16,256]{2,1,0:T(8,128)(2,1)}), bf16[8,16,256]{2,1,0:T(8,128)(2,1)S(1)}, u32[]{:S(2)}, u32[]{:S(2)}) %all-to-all-start.3) | async-done | bytes 65568 | tf_op jit(solution)/shard_map/all_to_all | solution.py:190
  225.2 0.5 gather_fusion.3
  225.9 9.3 %all_to_all.26 = bf16[8,16,256]{2,1,0:T(8,128)(2,1)S(1)} all-to-all(bf16[8,16,256]{2,1,0:T(8,128)(2,1)S(1)} %broadcast_select_fusion.2), channel_id=1, replica_groups=mesh['seq'=8,'head'=4] {'seq'}, dimensions={0} | all-to-all | bytes 131072 | tf_op jit(solution)/shard_map/all_to_all | solution.py:197
  235.2 0.6 copy.208
  (68 shorter events, 3.1 us)
Async XLA Ops:
  6.5 152.3 %copy-start = (bf16[2,1024,704]{1,2,0:T(8,128)(2,1)S(1)}, bf16[2,1024,704]{1,2,0:T(8,128)(2,1)}, u32[]{:S(2)}) copy-start(bf16[2,1024,704]{1,2,0:T(8,128)(2,1)} %param.30) | copy-start | bytes 8650756
  6.5 80.4 %all-reduce.2.cloned.1.call-start = ((), (), s32[]{:S(2)}) async-start(), calls=%async_computation.5 | async-start | bytes 1048576 | tf_op jit(solution)/shard_map/psum | solution.py:141
  7.4 8.0 %copy-start.8 = (pred[128]{0:T(512)(128)(4,1)}, pred[128]{0:T(512)(128)(4,1)S(1)}, u32[]{:S(2)}) copy-start(pred[128]{0:T(512)(128)(4,1)S(1)} %iota_compare_fusion.2) | copy-start | bytes 388
  50.3 1.0 copy-start.3
  50.5 1.1 copy-start.4
  50.7 1.7 copy-start.5
  51.6 36.5 %copy-start.7 = (f32[1024]{0:T(1024)S(1)}, f32[1024]{0:T(1024)}, u32[]{:S(2)}) copy-start(f32[1024]{0:T(1024)} %param.25) | copy-start | bytes 12292
  51.6 0.8 copy-start.2
  154.0 0.8 copy-start.1
  168.4 20.2 %all-to-all-start.1 = ((bf16[8,2,20,4,256]{4,3,2,1,0:T(4,128)(2,1)}), bf16[8,2,20,4,256]{4,3,2,1,0:T(4,128)(2,1)}, u32[]{:S(2)}, u32[]{:S(2)}) async-start(bf16[8,2,20,4,256]{4,3,2,1,0:T(4,128)(2,1)} %copy.154), calls=%async_computation.1 | async-start | bytes 1310720 | tf_op jit(solution)/shard_map/all_to_all | solution.py:170
  173.7 21.4 %copy-start.6 = (bf16[256,16]{0,1:T(8,128)(2,1)S(1)}, bf16[256,16]{0,1:T(8,128)(2,1)}, u32[]{:S(2)}) copy-start(bf16[256,16]{0,1:T(8,128)(2,1)} %param.26) | copy-start | bytes 24580
  190.9 18.4 %all-to-all-start.2 = ((bf16[8,2,20,4,256]{4,0,2,1,3:T(8,128)(2,1)}), bf16[8,2,20,4,256]{4,0,2,1,3:T(8,128)(2,1)}, u32[]{:S(2)}, u32[]{:S(2)}) async-start(bf16[8,2,20,4,256]{4,0,2,1,3:T(8,128)(2,1)} %copy.155), calls=%async_computation.2 | async-start | bytes 1310720 | tf_op jit(solution)/shard_map/all_to_all | solution.py:169
  210.7 2.3 copy-start.9
  214.7 10.6 %all-to-all-start.3 = ((bf16[8,16,256]{2,1,0:T(8,128)(2,1)}), bf16[8,16,256]{2,1,0:T(8,128)(2,1)S(1)}, u32[]{:S(2)}, u32[]{:S(2)}) async-start(bf16[8,16,256]{2,1,0:T(8,128)(2,1)} %bitcast.33), calls=%async_computation.3 | async-start | bytes 131072 | tf_op jit(solution)/shard_map/all_to_all | solution.py:190
Sparse Core Ops, SparseCore 0:
  52.6 34.3 all-reduce.1
where the time goes:
time: 245 us; the launch traced here: 243 us
  blocking collectives  76.4 us (31%)
  local copies, waits for them, and re-layouts  63.4 us (26%)
  waiting for transfers between devices  54.8 us (22%)
  between operations  14.6 us (6%)
  starting transfers between devices  12 us (5%)
  other arithmetic  11.3 us (5%)
  matrix products  10.1 us (4%)
    scatter x1, local copies, waits for them, and re-layouts, on_device(): send_rows.at[target_device, local_slot, slot_rank]  37.4 us
    all_gather x1, blocking collectives, on_device(): all_pages = lax.all_gather(local_pages, 'seq', axis=0, tiled=True)  33 us
    psum x1, waiting for transfers between devices, on_device(): resid = lax.psum(partial_proj, 'head')  32.9 us
    all_to_all x1, blocking collectives, on_device(): lax.all_to_all(send_rows, 'seq', split_axis=0, concat_axis=0, tiled=True)  22.2 us
    all_to_all x1, waiting for transfers between devices, on_device(): lax.all_to_all(split_part.astype(jnp.bfloat16), 'seq', split_axis=0, conc...  14.9 us
    psum x1, blocking collectives, on_device(): lax.psum(jnp.dot(normed_columns, router_weight, preferred_element_type=jn...  11.9 us
    all_to_all x1, blocking collectives, on_device(): lax.all_to_all(reordered, 'seq', split_axis=0, concat_axis=0, tiled=True)  9.29 us
    unnamed x28, local copies, waits for them, and re-layouts  7.66 us
  transfers between devices with their start and end apart: 4, of which 3 were waited for; matrix products, arithmetic and copies ran while one was open for 2% of the time, Pallas kernels for 0%

commit v1 on v0

v1 whole, which is shorter than its diff:
```python
import functools

import jax
import jax.numpy as jnp
from jax import lax
from jax.experimental import pallas as pl
from jax.experimental.pallas import tpu as pltpu
from jax.sharding import PartitionSpec as P

DH = 64
EXPERTS = 16
TOPK = 2
GROUPS = 4
norm_eps = 1e-06

F32, BF16, I32 = jnp.float32, jnp.bfloat16, jnp.int32
NT = (((1,), (1,)), ((), ()))
TN = (((0,), (0,)), ((), ()))


def mm(a, b, dims=(((1,), (0,)), ((), ()))):
    return lax.dot_general(a, b, dims, preferred_element_type=F32)


def iota(shape, dim):
    return lax.broadcasted_iota(I32, shape, dim)


def remote(src, dst, send, recv, **where):
    return pltpu.make_async_remote_copy(
        src_ref=src,
        dst_ref=dst,
        send_sem=send,
        recv_sem=recv,
        device_id=where,
        device_id_type=pl.DeviceIdType.MESH,
    )


def each(low, high, step):
    if high - low <= 16:
        for i in range(low, high):
            step(i)
        return

    def body(i, carry):
        step(i)
        return carry

    lax.fori_loop(low, high, body, 0)


def layer_kernel(
    cfg,
    lengths,
    page_group,
    destinations,
    hidden,
    queries,
    keys,
    values,
    key_cache,
    value_cache,
    out_weight,
    gain,
    router,
    routes,
    gate_hbm,
    up_hbm,
    down_hbm,
    out,
    gate_w,
    up_w,
    down_w,
    key_pages,
    value_pages,
    ow,
    att,
    squares,
    diffs,
    send_rows,
    slots,
    partial,
    pair_send,
    pair_recv,
    cross_send,
    cross_recv,
    home_send,
    returned,
    piece_send,
    pieces,
    place_send,
    placed,
    weight_sem,
    page_sem,
    head_sem,
    seq_sem,
    fwd_sem,
    back_sem,
):
    S, H, per_device, replicas, capacity, pair_rows, inside = cfg
    me, h = lax.axis_index("seq"), lax.axis_index("head")
    rows, cols = hidden.shape
    page_local, page_rows, _ = key_cache.shape
    slot_rows = S * pair_rows
    pair = h + 1 - 2 * (h % 2)
    cross = (h + 2) % 4

    loads = [
        pltpu.make_async_copy(a, b, weight_sem.at[i])
        for i, (a, b) in enumerate(((gate_hbm, gate_w), (up_hbm, up_w), (down_hbm, down_w)))
    ]
    for load in loads:
        load.start()

    barrier = pltpu.get_barrier_semaphore()
    each(
        1,
        S,
        lambda i: pl.semaphore_signal(
            barrier, inc=1, device_id={"seq": (me + i) % S}, device_id_type=pl.DeviceIdType.MESH
        ),
    )
    for j in range(1, H):
        pl.semaphore_signal(
            barrier, inc=1, device_id={"head": (h + j) % H}, device_id_type=pl.DeviceIdType.MESH
        )
    pl.semaphore_wait(barrier, S - 1 + H - 1)

    def page_copy(i, which):
        src, dst = ((key_cache, key_pages), (value_cache, value_pages))[which]
        return remote(
            src,
            dst.at[pl.ds(me * page_local, page_local)],
            page_sem.at[which, 0, i],
            page_sem.at[which, 1, i],
            seq=(me + i) % S,
        )

    def start_pages(i):
        page_copy(i, 0).start()
        page_copy(i, 1).start()

    each(1, S, start_pages)
    key_pages[pl.ds(me * page_local, page_local)] = key_cache[...]
    value_pages[pl.ds(me * page_local, page_local)] = value_cache[...]

    def head_copy(kind, j):
        to = (h + j) % H
        src, dst = (
            (out_weight.at[:, pl.ds(pl.multiple_of(to * cols, cols), cols)], ow.at[h]),
            (att.at[h], att.at[h]),
            (squares.at[h], squares.at[h]),
            (diffs.at[h], diffs.at[h]),
        )[kind]
        return remote(src, dst, head_sem.at[kind, 0, j], head_sem.at[kind, 1, j], head=to)

    for j in range(1, H):
        head_copy(0, j).start()
    ow[h] = out_weight[:, pl.ds(pl.multiple_of(h * cols, cols), cols)]

    eye = iota((rows, rows), 0) == iota((rows, rows), 1)

    def as_row(column):
        row = jnp.sum(jnp.where(eye, column, 0.0), axis=0, keepdims=True)
        return jnp.broadcast_to(row, (8, rows))

    def as_column(row):
        return jnp.sum(jnp.where(eye, row, 0.0), axis=1, keepdims=True)

    expert = iota((rows, EXPERTS), 1)
    named = routes[...].astype(F32)
    is_first = (as_column(named[0:1]).astype(I32) == expert).astype(F32)
    is_second = (as_column(named[1:2]).astype(I32) == expert).astype(F32)
    sub_rows = rows // replicas
    before = (iota((rows, rows), 1) < iota((rows, rows), 0)) & (
        iota((rows, rows), 1) // sub_rows == iota((rows, rows), 0) // sub_rows
    )
    rank = mm(before.astype(F32).astype(BF16), (is_first + is_second).astype(BF16))
    target = expert // per_device * replicas + iota((rows, EXPERTS), 0) // sub_rows
    slot = (target * pair_rows + expert % per_device * capacity).astype(F32) + rank
    slot_of = [
        jnp.sum(one * slot, axis=1, keepdims=True).astype(I32) for one in (is_first, is_second)
    ]
    slot_ids = iota((rows, slot_rows), 1)
    choose = [(slot_ids == s).astype(F32).astype(BF16) for s in slot_of]

    heads = cols // DH
    lane_head = iota((rows, cols), 1) // DH
    query = queries[...]
    stacked = jnp.concatenate(
        [jnp.where(lane_head == n, query, jnp.zeros_like(query)) for n in range(heads)], axis=0
    )
    scale = DH ** (-0.5)
    suffix = mm(stacked, keys[...], NT) * scale
    position = iota((heads * rows, rows), 0) % rows
    key_position = iota((heads * rows, rows), 1)
    suffix = jnp.where(
        (key_position <= position) & (key_position < lengths[0]), suffix, -jnp.inf
    )

    group = me // (S // GROUPS)

    lane_page = iota((1, S * page_local * page_rows), 1) // page_rows

    def mark(p, held):
        return jnp.where((lane_page == p) & (page_group[p] == group), 1.0, held)

    ours = lax.fori_loop(0, S * page_local, mark, jnp.zeros(lane_page.shape, F32))

    def wait_pages(i):
        page_copy(i, 0).wait_recv()
        page_copy(i, 1).wait_recv()

    each(1, S, wait_pages)
    prefix_keys = key_pages[...].reshape(-1, cols)
    prefix_values = value_pages[...].reshape(-1, cols)
    prefix = jnp.where(ours > 0.5, mm(stacked, prefix_keys, NT) * scale, -jnp.inf)
    top = jnp.maximum(
        jnp.max(prefix, axis=1, keepdims=True), jnp.max(suffix, axis=1, keepdims=True)
    )
    prefix = jnp.exp(prefix - top)
    suffix = jnp.exp(suffix - top)
    total = jnp.sum(prefix, axis=1, keepdims=True) + jnp.sum(suffix, axis=1, keepdims=True)
    mixed = mm((prefix / total).astype(BF16), prefix_values) + mm(
        (suffix / total).astype(BF16), values[...]
    )
    attended = jnp.zeros((rows, cols), F32)
    for n in range(heads):
        attended = jnp.where(lane_head == n, mixed[n * rows : (n + 1) * rows], attended)
    att[h] = attended.astype(BF16)
    for j in range(1, H):
        head_copy(1, j).start()
    for j in range(1, H):
        head_copy(0, j).wait_recv()
    for j in range(1, H):
        head_copy(1, j).wait_recv()
    resid = hidden[...].astype(F32)
    for j in range(H):
        resid = resid + mm(att[j], ow[j])

    squares[h] = as_row(jnp.sum(resid * resid, axis=1, keepdims=True))
    for j in range(1, H):
        head_copy(2, j).start()
    for j in range(1, H):
        head_copy(2, j).wait_recv()
    square = as_column((squares[0] + squares[1] + squares[2] + squares[3])[0:1])
    normed = (
        resid * lax.rsqrt(square / (H * cols) + norm_eps) * gain[pl.ds(h, 1), :]
    ).astype(BF16)

    send_rows[...] = mm(choose[0] + choose[1], normed, TN).astype(BF16)

    def block(s):
        return pl.ds(pl.multiple_of(s * pair_rows, pair_rows), pair_rows)

    def dispatch(i):
        to = (me + i) % S
        return remote(
            send_rows.at[block(to)],
            slots.at[h, block(me)],
            seq_sem.at[0, 0, i],
            seq_sem.at[0, 1, i],
            seq=to,
        )

    each(1, S, lambda i: dispatch(i).start())
    slots[h, block(me)] = send_rows[block(me)]

    def forward(kind, i):
        source = (me + S - i) % S
        held = slots.at[cross if kind == 2 else h, block(source)]
        return remote(
            held,
            held,
            fwd_sem.at[kind, 0, i],
            fwd_sem.at[kind, 1, i],
            head=cross if kind == 1 else pair,
        )

    forward(1, 0).start()
    forward(0, 0).start()
    logits = mm(normed, router[...], NT)
    diffs[h] = as_row(jnp.sum((is_first - is_second) * logits, axis=1, keepdims=True))
    for j in range(1, H):
        head_copy(3, j).start()

    def pass_on(i):
        dispatch(i).wait_recv()
        forward(1, i).start()
        forward(0, i).start()

    each(1, S, pass_on)

    def pass_across(i):
        forward(1, i).wait_recv()
        forward(2, i).start()

    each(0, S, pass_across)
    for load in loads:
        load.wait()

    def wait_forward(i):
        forward(0, i).wait_recv()
        forward(2, i).wait_recv()

    each(0, S, wait_forward)

    def expert_rows(p, parts):
        gate_act = sum(mm(parts[j], gate_w[p, :, j * cols : (j + 1) * cols], NT) for j in range(H))
        up_act = sum(mm(parts[j], up_w[p, :, j * cols : (j + 1) * cols], NT) for j in range(H))
        inner = 0.7978845608028654 * (gate_act + 0.044715 * gate_act * gate_act * gate_act)
        act = (0.5 * gate_act * (1.0 + jnp.tanh(inner)) * up_act).astype(BF16)
        return [mm(act, down_w[p, :, j * cols : (j + 1) * cols]) for j in range(H)]

    if per_device == 1:
        chunk = min(256, slot_rows)

        def one_chunk(i):
            at = pl.ds(pl.multiple_of(i * chunk, chunk), chunk)
            done = expert_rows(0, [slots[j, at] for j in range(H)])
            for j in range(H):
                partial[j, at] = done[j]

        each(0, slot_rows // chunk, one_chunk)
    else:
        own = S * capacity
        row, column = iota((own, slot_rows), 0), iota((own, slot_rows), 1)
        for p in range(per_device):
            pick = (
                (column == row // capacity * pair_rows + p * capacity + row % capacity)
                .astype(F32)
                .astype(BF16)
            )
            done = expert_rows(p, [mm(pick, slots[j]).astype(BF16) for j in range(H)])
            for j in range(H):
                back = mm(pick, done[j].astype(BF16), TN)
                partial[j] = back if p == 0 else partial[j] + back

    pair_send[0] = partial[pair].astype(BF16)
    pair_send[1] = partial[(pair + 2) % 4].astype(BF16)
    pair_copies = [
        remote(
            pair_send.at[n],
            pair_recv.at[n],
            back_sem.at[0, 0, n],
            back_sem.at[0, 1, n],
            head=pair,
        )
        for n in range(2)
    ]
    pair_copies[1].start()
    pair_copies[0].start()
    pair_copies[1].wait_recv()
    cross_send[...] = (partial[cross] + pair_recv[1].astype(F32)).astype(BF16)

    def cross_copy(i):
        at = block((me + i) % S)
        return remote(
            cross_send.at[at],
            cross_recv.at[at],
            back_sem.at[1, 0, i],
            back_sem.at[1, 1, i],
            head=cross,
        )

    each(1, S + 1, lambda i: cross_copy(i).start())
    pair_copies[0].wait_recv()

    def home_copy(i):
        to = (me + i) % S
        return remote(
            home_send.at[block(to)],
            returned.at[block(me)],
            seq_sem.at[1, 0, i],
            seq_sem.at[1, 1, i],
            seq=to,
        )

    def total_block(i):
        at = block((me + i) % S)
        cross_copy(i).wait_recv()
        return (
            partial[h, at] + pair_recv[0, at].astype(F32) + cross_recv[at].astype(F32)
        ).astype(BF16)

    def send_home(i):
        home_send[block((me + i) % S)] = total_block(i)
        home_copy(i).start()

    each(1, S, send_home)
    returned[block(me)] = total_block(S)
    for j in range(1, H):
        head_copy(3, j).wait_recv()
    difference = as_column((diffs[0] + diffs[1] + diffs[2] + diffs[3])[0:1])
    gate_first = 1.0 / (1.0 + jnp.exp(-difference))
    gate_second = 1.0 / (1.0 + jnp.exp(difference))
    each(1, S, lambda i: home_copy(i).wait_recv())
    back = returned[...]
    layer = resid + gate_first * mm(choose[0], back) + gate_second * mm(choose[1], back)
    layer = jnp.where(iota((rows, cols), 0) < lengths[0], layer, 0.0).astype(BF16)

    if not inside:
        out[...] = layer
    else:
        piece = rows // S

        def part(s):
            return pl.ds(pl.multiple_of(s * piece, piece), piece)

        def out_copy(stage, i):
            to = (me + i) % S
            src, dst = ((piece_send, pieces), (place_send, placed))[stage]
            return remote(
                src.at[part(to)],
                dst.at[me] if stage == 0 else dst.at[part(me)],
                seq_sem.at[2 + stage, 0, i],
                seq_sem.at[2 + stage, 1, i],
                seq=to,
            )

        piece_send[...] = layer
        each(1, S, lambda i: out_copy(0, i).start())
        pieces[me] = piece_send[part(me)]
        origin = []
        for d in range(S):
            r = jnp.int32(0)
            for n in range(S):
                r = jnp.where(destinations[n] == d, n, r)
            origin.append(r)
        each(1, S, lambda i: out_copy(0, i).wait_recv())
        for d in range(S):
            taken = jnp.zeros((piece, cols), F32)
            for n in range(S):
                taken = jnp.where(origin[d] == n, pieces[n].astype(F32), taken)
            place_send[d * piece : (d + 1) * piece] = taken.astype(BF16)
        each(1, S, lambda i: out_copy(1, i).start())
        placed[part(me)] = place_send[part(me)]
        each(1, S, lambda i: out_copy(1, i).wait_recv())
        out[...] = placed[...]

    def sent(i):
        page_copy(i, 0).wait_send()
        page_copy(i, 1).wait_send()
        dispatch(i).wait_send()
        home_copy(i).wait_send()
        if inside:
            out_copy(0, i).wait_send()
            out_copy(1, i).wait_send()

    each(1, S, sent)

    def sent_all(i):
        for kind in range(3):
            forward(kind, i).wait_send()
        cross_copy(i + 1).wait_send()

    each(0, S, sent_all)
    for j in range(1, H):
        for kind in range(4):
            head_copy(kind, j).wait_send()
    for n in range(2):
        pair_copies[n].wait_send()


def on_device(
    hidden,
    queries,
    suffix_keys,
    suffix_values,
    lengths,
    key_cache,
    value_cache,
    page_group,
    out_weight,
    norm_gain,
    router_weight,
    routes,
    gate_weight,
    up_weight,
    down_weight,
    destinations,
):
    S, H = lax.axis_size("seq"), lax.axis_size("head")
    rows, cols = hidden.shape
    replicas = max(1, S // EXPERTS)
    per_device = max(1, EXPERTS // S)
    least = 5 * rows * TOPK // (4 * EXPERTS * replicas)
    unit = 16 // min(per_device, 2)
    capacity = -(-least // unit) * unit
    pair_rows = per_device * capacity
    slot_rows = S * pair_rows
    inside = rows % (16 * S) == 0
    pages = S * key_cache.shape[0]
    page_shape = (pages, *key_cache.shape[1:])
    small = rows if inside else 16

    def vmem(*shape, dtype=BF16):
        return pltpu.VMEM(shape, dtype)

    dma = pltpu.SemaphoreType.DMA
    whole = pl.BlockSpec(memory_space=pltpu.VMEM)
    scalars = pl.BlockSpec(memory_space=pltpu.SMEM)
    hbm = pl.BlockSpec(memory_space=pl.ANY)
    gate_weight, up_weight, down_weight = (
        jnp.swapaxes(w, 1, 2) for w in (gate_weight, up_weight, down_weight)
    )
    layer = pl.pallas_call(
        functools.partial(
            layer_kernel, (S, H, per_device, replicas, capacity, pair_rows, inside)
        ),
        out_shape=jax.ShapeDtypeStruct((rows, cols), BF16),
        in_specs=[scalars] * 3 + [whole] * 10 + [hbm] * 3,
        out_specs=whole,
        scratch_shapes=[
            vmem(*gate_weight.shape),
            vmem(*up_weight.shape),
            vmem(*down_weight.shape),
            vmem(*page_shape),
            vmem(*page_shape),
            vmem(H, cols, cols),
            vmem(H, rows, cols),
            vmem(H, 8, rows, dtype=F32),
            vmem(H, 8, rows, dtype=F32),
            vmem(slot_rows, cols),
            vmem(H, slot_rows, cols),
            vmem(H, slot_rows, cols, dtype=F32),
            vmem(2, slot_rows, cols),
            vmem(2, slot_rows, cols),
            vmem(slot_rows, cols),
            vmem(slot_rows, cols),
            vmem(slot_rows, cols),
            vmem(slot_rows, cols),
            vmem(small, cols),
            vmem(S if inside else 1, max(16, rows // S), cols),
            vmem(small, cols),
            vmem(small, cols),
            dma((3,)),
            dma((2, 2, S)),
            dma((4, 2, H)),
            dma((4, 2, S)),
            dma((3, 2, S)),
            dma((2, 2, S + 1)),
        ],
        compiler_params=pltpu.CompilerParams(
            collective_id=0, has_side_effects=True, vmem_limit_bytes=56 * 2**20
        ),
    )(
        lengths,
        page_group,
        destinations,
        hidden,
        queries,
        suffix_keys,
        suffix_values,
        key_cache,
        value_cache,
        out_weight,
        norm_gain.reshape(H, cols),
        router_weight.T,
        routes.T,
        gate_weight,
        up_weight,
        down_weight,
    )
    if inside:
        return layer
    out_pieces = layer.reshape(S, rows // S, cols)
    scattered = lax.all_to_all(out_pieces, "seq", split_axis=0, concat_axis=0, tiled=True)
    index = jnp.arange(S, dtype=I32)
    origin = jnp.sum(jnp.where(destinations[None, :] == index[:, None], index[None, :], 0), axis=1)
    chosen = (origin[:, None] == index[None, :]).astype(BF16)
    reordered = jnp.dot(chosen, scattered.reshape(S, -1), preferred_element_type=F32)
    reordered = reordered.astype(BF16).reshape(scattered.shape)
    settled = lax.all_to_all(reordered, "seq", split_axis=0, concat_axis=0, tiled=True)
    return settled.reshape(rows, cols)


def solution(mesh):
    return jax.shard_map(
        on_device,
        mesh=mesh,
        in_specs=(
            P("seq", "head"),
            P("seq", "head"),
            P("seq", "head"),
            P("seq", "head"),
            P("seq"),
            P("seq", None, "head"),
            P("seq", None, "head"),
            P(),
            P("head", None),
            P(),
            P("head", None),
            P("seq", None),
            P("seq", None, "head"),
            P("seq", None, "head"),
            P("seq", None, "head"),
            P(),
        ),
        out_specs=P("seq", "head"),
        check_vma=False,
    )
```

time: 245 us -> 61.9 us (0.25)
  blocking collectives: 76.4 us -> 0 us
  local copies, waits for them, and re-layouts: 63.4 us -> 2.76 us
  Pallas kernels: 0 us -> 58.3 us
  waiting for transfers between devices: 54.8 us -> 0 us
  between operations: 14.6 us -> 0.66 us
  starting transfers between devices: 12 us -> 0 us
  other arithmetic: 11.3 us -> 0 us
  matrix products: 10.1 us -> 0 us
    pallas_call x0 -> x1, Pallas kernels: none -> 58.3 us  [on_device(): pl.pallas_call(functools.partial(layer_kernel, (S, H, per_device, replica...]
    scatter x3 -> x0, local copies, waits for them, and re-layouts: 38.7 us -> none  [the longest x1 37.4 us: on_device(): send_rows.at[target_device, local_slot, slot_rank]]
    all_gather x1 -> x0, blocking collectives: 33 us -> none  [on_device(): all_pages = lax.all_gather(local_pages, 'seq', axis=0, tiled=True)]
    psum x1 -> x0, waiting for transfers between devices: 32.9 us -> none  [on_device(): resid = lax.psum(partial_proj, 'head')]
    all_to_all x2 -> x0, blocking collectives: 31.5 us -> none  [the longest x1 22.2 us: on_device(): lax.all_to_all(send_rows, 'seq', split_axis=0, concat_axis=0, tiled=True)]
    all_to_all x3 -> x0, waiting for transfers between devices: 21.8 us -> none  [the longest x1 14.9 us: on_device(): lax.all_to_all(split_part.astype(jnp.bfloat16), 'seq', split_axis=0, conc...]
    all_to_all x3 -> x0, starting transfers between devices: 12 us -> none  [the longest x1 4.19 us: on_device(): lax.all_to_all(split_part.astype(jnp.bfloat16), 'seq', split_axis=0, conc...]
    psum x1 -> x0, blocking collectives: 11.9 us -> none  [on_device(): lax.psum(jnp.dot(normed_columns, router_weight, preferred_element_type=jn...]
  transfers between devices with their start and end apart: 4 -> 0, of which waited for: 3 -> 0; matrix products, arithmetic and copies ran while one was open for 2% -> 0% of each run, Pallas kernels for 0% -> 0%
where the time goes in v1:
time: 61.9 us; the launch traced here: 61.7 us
  Pallas kernels  58.3 us (94%)
  local copies, waits for them, and re-layouts  2.76 us (4%)
  between operations  0.66 us (1%)
    pallas_call x1, Pallas kernels, on_device(): pl.pallas_call(functools.partial(layer_kernel, (S, H, per_device, replica...  58.3 us
    unnamed x1, local copies, waits for them, and re-layouts  1.47 us
    reshape x1, local copies, waits for them, and re-layouts, on_device(): norm_gain.reshape(H, cols)  1.29 us

profile of v1, /device:TPU:0, one launch (start us, length us, event | category | flops | bytes accessed | tf_op | source)
XLA Modules:
  0.0 61.7 jit_solution(17025632762556234289)
XLA Ops:
  0.7 1.3 %reshape.3.gain = f32[4,256]{1,0:T(4,128)} reshape(f32[1024]{0:T(1024)} %param.25) | data formatting | bytes 8192 | tf_op jit(solution)/shard_map/reshape | solution.py:559
  1.9 58.3 %shard_map.154 = bf16[128,256]{1,0:T(8,128)(2,1)} custom-call(s32[1]{0:T(128)S(6)} %copy.18.lengths, s32[8]{0:T(128)} %page_group.1, s32[8]{0:T(128)} %destinations.1, bf16[128,256]{1,0:T(8,128)(2,1)} %hidden.1, bf16[128,256]{1,0:T(8,128)(2,1)} %queries.1, bf16[128,256]{1,0:T(8,128)(2,1)} %keys.1, bf16[128,256]{1,0:T(8,128)(2,1)} %values.1, ...), custom_call_target="tpu_custom_call" | custom-call | tf_op jit(solution)/shard_map/pallas_call | solution.py:508
  60.2 1.5 %copy.19 = bf16[128,256]{1,0:T(8,128)(2,1)} copy(bf16[128,256]{1,0:T(8,128)(2,1)} %shard_map.154) | data formatting | bytes 131072

commit v2 on v1

--- a/solution.py
+++ b/solution.py
@@ -127,6 +127,9 @@
         )
     pl.semaphore_wait(barrier, S - 1 + H - 1)
 
+    def columns(b):
+        return pl.ds(pl.multiple_of(b * cols, cols), cols)
+
     def page_copy(i, which):
         src, dst = ((key_cache, key_pages), (value_cache, value_pages))[which]
         return remote(
@@ -246,7 +249,7 @@
         head_copy(2, j).wait_recv()
     square = as_column((squares[0] + squares[1] + squares[2] + squares[3])[0:1])
     normed = (
-        resid * lax.rsqrt(square / (H * cols) + norm_eps) * gain[pl.ds(h, 1), :]
+        resid * lax.rsqrt(square / (H * cols) + norm_eps) * gain[:, columns(h)]
     ).astype(BF16)
 
     send_rows[...] = mm(choose[0] + choose[1], normed, TN).astype(BF16)
@@ -290,55 +293,72 @@
         forward(1, i).start()
         forward(0, i).start()
 
+    for load in loads:
+        load.wait()
     each(1, S, pass_on)
 
     def pass_across(i):
         forward(1, i).wait_recv()
         forward(2, i).start()
 
-    each(0, S, pass_across)
-    for load in loads:
-        load.wait()
-
-    def wait_forward(i):
-        forward(0, i).wait_recv()
-        forward(2, i).wait_recv()
-
-    each(0, S, wait_forward)
-
-    def expert_rows(p, parts):
-        gate_act = sum(mm(parts[j], gate_w[p, :, j * cols : (j + 1) * cols], NT) for j in range(H))
-        up_act = sum(mm(parts[j], up_w[p, :, j * cols : (j + 1) * cols], NT) for j in range(H))
+    def activate(gate_act, up_act):
         inner = 0.7978845608028654 * (gate_act + 0.044715 * gate_act * gate_act * gate_act)
-        act = (0.5 * gate_act * (1.0 + jnp.tanh(inner)) * up_act).astype(BF16)
-        return [mm(act, down_w[p, :, j * cols : (j + 1) * cols]) for j in range(H)]
-
+        return (0.5 * gate_act * (1.0 + jnp.tanh(inner)) * up_act).astype(BF16)
+
+    last = (pair + 2) % 4
     if per_device == 1:
+        each(0, S, pass_across)
+        each(0, S, lambda i: forward(0, i).wait_recv())
+        each(0, S, lambda i: forward(2, i).wait_recv())
         chunk = min(256, slot_rows)
 
         def one_chunk(i):
             at = pl.ds(pl.multiple_of(i * chunk, chunk), chunk)
-            done = expert_rows(0, [slots[j, at] for j in range(H)])
+            gate_act, up_act = (
+                sum(mm(slots[j, at], w[0, :, j * cols : (j + 1) * cols], NT) for j in range(H))
+                for w in (gate_w, up_w)
+            )
+            act = activate(gate_act, up_act)
             for j in range(H):
-                partial[j, at] = done[j]
+                partial[j, at] = mm(act, down_w[0, :, j * cols : (j + 1) * cols])
 
         each(0, slot_rows // chunk, one_chunk)
+
+        def block_out(b):
+            return partial[b]
+
     else:
         own = S * capacity
         row, column = iota((own, slot_rows), 0), iota((own, slot_rows), 1)
-        for p in range(per_device):
-            pick = (
-                (column == row // capacity * pair_rows + p * capacity + row % capacity)
-                .astype(F32)
-                .astype(BF16)
+        picks = [
+            (column == row // capacity * pair_rows + p * capacity + row % capacity)
+            .astype(F32)
+            .astype(BF16)
+            for p in range(per_device)
+        ]
+        sums = [None] * per_device
+
+        def feed(b):
+            for p in range(per_device):
+                x = mm(picks[p], slots[b]).astype(BF16)
+                more = [mm(x, w[p, :, columns(b)], NT) for w in (gate_w, up_w)]
+                sums[p] = more if sums[p] is None else [m + n for m, n in zip(sums[p], more)]
+
+        feed(h)
+        each(0, S, pass_across)
+        each(0, S, lambda i: forward(0, i).wait_recv())
+        feed(pair)
+        feed(cross)
+        each(0, S, lambda i: forward(2, i).wait_recv())
+        feed(last)
+        acts = [activate(*sums[p]) for p in range(per_device)]
+
+        def block_out(b):
+            return sum(
+                mm(picks[p], mm(acts[p], down_w[p, :, columns(b)]).astype(BF16), TN)
+                for p in range(per_device)
             )
-            done = expert_rows(p, [mm(pick, slots[j]).astype(BF16) for j in range(H)])
-            for j in range(H):
-                back = mm(pick, done[j].astype(BF16), TN)
-                partial[j] = back if p == 0 else partial[j] + back
-
-    pair_send[0] = partial[pair].astype(BF16)
-    pair_send[1] = partial[(pair + 2) % 4].astype(BF16)
+
     pair_copies = [
         remote(
             pair_send.at[n],
@@ -349,10 +369,11 @@
         )
         for n in range(2)
     ]
+    pair_send[1] = block_out(last).astype(BF16)
     pair_copies[1].start()
-    pair_copies[0].start()
+    crossing = block_out(cross)
     pair_copies[1].wait_recv()
-    cross_send[...] = (partial[cross] + pair_recv[1].astype(F32)).astype(BF16)
+    cross_send[...] = (crossing + pair_recv[1].astype(F32)).astype(BF16)
 
     def cross_copy(i):
         at = block((me + i) % S)
@@ -365,6 +386,9 @@
         )
 
     each(1, S + 1, lambda i: cross_copy(i).start())
+    pair_send[0] = block_out(pair).astype(BF16)
+    pair_copies[0].start()
+    partial[h] = block_out(h)
     pair_copies[0].wait_recv()
 
     def home_copy(i):
@@ -556,7 +580,7 @@
         key_cache,
         value_cache,
         out_weight,
-        norm_gain.reshape(H, cols),
+        norm_gain.reshape(1, H * cols),
         router_weight.T,
         routes.T,
         gate_weight,

time: 61.9 us -> 59.6 us (0.963)
  local copies, waits for them, and re-layouts: 2.76 us -> 1.47 us
  Pallas kernels: 58.3 us -> 57.3 us
    reshape x1 -> x0, local copies, waits for them, and re-layouts: 1.29 us -> none  [on_device(): norm_gain.reshape(H, cols)]
    pallas_call x1, Pallas kernels: 58.3 us -> 57.3 us  [on_device(): pl.pallas_call(functools.partial(layer_kernel, (S, H, per_device, replica...]
where the time goes in v2:
time: 59.6 us; the launch traced here: 59.4 us
  Pallas kernels  57.3 us (96%)
  local copies, waits for them, and re-layouts  1.47 us (2%)
  between operations  0.66 us (1%)
    pallas_call x1, Pallas kernels, on_device(): pl.pallas_call(functools.partial(layer_kernel, (S, H, per_device, replica...  57.3 us
    unnamed x1, local copies, waits for them, and re-layouts  1.47 us

profile of v2, /device:TPU:0, one launch (start us, length us, event | category | flops | bytes accessed | tf_op | source)
XLA Modules:
  0.0 59.4 jit_solution(5991164142576933942)
XLA Ops:
  0.7 57.3 %shard_map.154 = bf16[128,256]{1,0:T(8,128)(2,1)} custom-call(s32[1]{0:T(128)S(6)} %copy.18.lengths, s32[8]{0:T(128)} %page_group.1, s32[8]{0:T(128)} %destinations.1, bf16[128,256]{1,0:T(8,128)(2,1)} %hidden.1, bf16[128,256]{1,0:T(8,128)(2,1)} %queries.1, bf16[128,256]{1,0:T(8,128)(2,1)} %keys.1, bf16[128,256]{1,0:T(8,128)(2,1)} %values.1, ...), custom_call_target="tpu_custom_call" | custom-call | tf_op jit(solution)/shard_map/pallas_call | solution.py:532
  57.9 1.5 %copy.19 = bf16[128,256]{1,0:T(8,128)(2,1)} copy(bf16[128,256]{1,0:T(8,128)(2,1)} %shard_map.154) | data formatting | bytes 131072
